TPU v7x, 128 devices: a whole 4x4x4 slice. The times are simulated.
128 devices in a mesh: store: 8 (over x, core), sku: 16 (over z, y).
Axes of the slice: x: 4, y: 4, z: 4, core: 2. Of those that a mesh axis runs over, the one named last changes fastest.
Arguments:
- base_bottom: float32 [128, 13, 16384], P(('store', 'sku')), may hold values from -6 to 6
- weight_bottom: float32 [128, 13, 16384], P(('store', 'sku')), may hold values from 0.5 to 4
- base_category: float32 [128, 13, 1024], P(('store', 'sku')), may hold values from -24 to 24
- weight_category: float32 [128, 13, 1024], P(('store', 'sku')), may hold values from 0.02 to 0.2
- base_region: float32 [32, 13, 16384], P(None, None, ('store', 'sku')), may hold values from -24 to 24
- weight_region: float32 [32, 13, 16384], P(None, None, ('store', 'sku')), may hold values from 0.02 to 0.2
- category_map: int32 [16384], replicated, may hold values from 0 to 1023
- region_map: int32 [128], replicated, may hold values from 0 to 31
Outputs:
- reconciled: float32 [128, 13, 16384], P(('store', 'sku'))
- residual: float32 [128, 13, 16384], P(('store', 'sku'))
All inputs are finite; a program needn't handle non-finite values.
Results may differ from a plain program's by a relative error of at most 0.0003.
Values sent between devices are 32-bit elements; how exact they have to be, the bound alone decides.
A program may use at most 128 MiB of HBM per device.

v0:
```python
import math
import jax
import jax.numpy as jnp
from jax import lax
from jax.sharding import PartitionSpec as P

ITERS = 3


def table_times(table, values):
    return jnp.dot(
        table, values, precision=lax.Precision.HIGHEST, preferred_element_type=jnp.float32
    )


def category_sums(field, category_map, n_cat):
    stores, horizon, skus = field.shape
    rows = stores * horizon
    flat = field.reshape(rows, skus)
    width = math.gcd(skus, 2048)
    labels = jnp.arange(n_cat, dtype=jnp.int32)

    def accumulate(blocknum, total):
        start = blocknum * width
        columns = lax.dynamic_slice_in_dim(flat, start, width, 1)
        members = lax.dynamic_slice_in_dim(category_map, start, width, 0)
        onehot = (members[:, None] == labels[None, :]).astype(jnp.float32)
        return total + jnp.dot(
            columns, onehot, precision=lax.Precision.HIGHEST, preferred_element_type=jnp.float32
        )

    total = lax.fori_loop(0, skus // width, accumulate, jnp.zeros((rows, n_cat), jnp.float32))
    return total.reshape(stores, horizon, n_cat)


def category_spread(values, category_map, skus):
    stores, horizon, n_cat = values.shape
    rows = stores * horizon
    flat = values.reshape(rows, n_cat)
    width = math.gcd(skus, 2048)
    labels = jnp.arange(n_cat, dtype=jnp.int32)

    def place(blocknum, output):
        start = blocknum * width
        members = lax.dynamic_slice_in_dim(category_map, start, width, 0)
        onehot = (labels[:, None] == members[None, :]).astype(jnp.float32)
        block = jnp.dot(
            flat, onehot, precision=lax.Precision.HIGHEST, preferred_element_type=jnp.float32
        )
        return lax.dynamic_update_slice_in_dim(output, block, start, 1)

    output = lax.fori_loop(0, skus // width, place, jnp.zeros((rows, skus), jnp.float32))
    return output.reshape(stores, horizon, skus)


def to_region(field):
    return lax.all_to_all(field, ("store", "sku"), split_axis=2, concat_axis=0, tiled=True)


def from_region(field):
    return lax.all_to_all(field, ("store", "sku"), split_axis=0, concat_axis=2, tiled=True)


def squares(residual):
    return lax.psum(jnp.sum(residual * residual), ("store", "sku"))


def on_device(
    base_bottom,
    weight_bottom,
    base_category,
    weight_category,
    base_region,
    weight_region,
    category_map,
    region_map,
):
    n_cat = weight_category.shape[2]
    n_regions, horizon, sku_local = weight_region.shape
    skus = base_bottom.shape[2]
    all_stores = region_map.shape[0]
    region_ids = jnp.arange(n_regions, dtype=jnp.int32)
    gather_table = (region_ids[:, None] == region_map[None, :]).astype(jnp.float32)
    spread_table = (region_map[:, None] == region_ids[None, :]).astype(jnp.float32)

    def region_sums(field):
        moved = to_region(field).reshape(all_stores, horizon * sku_local)
        summed = table_times(gather_table, moved)
        return summed.reshape(n_regions, horizon, sku_local)

    def spread_both(cat_values, region_values):
        flat = region_values.reshape(n_regions, horizon * sku_local)
        spread = table_times(spread_table, flat)
        returned = from_region(spread.reshape(all_stores, horizon, sku_local))
        return category_spread(cat_values, category_map, skus) + returned

    reconciled = base_bottom
    region_start = weight_region * (base_region - region_sums(base_bottom))
    cat_start = weight_category * (base_category - category_sums(base_bottom, category_map, n_cat))
    residual = spread_both(cat_start, region_start)
    direction = residual
    norm_now = squares(residual)
    for repeat in range(ITERS):
        operate_region_values = weight_region * region_sums(direction)
        operate_cat_values = weight_category * category_sums(direction, category_map, n_cat)
        image = weight_bottom * direction + spread_both(operate_cat_values, operate_region_values)
        step_size = norm_now / lax.psum(jnp.sum(direction * image), ("store", "sku"))
        reconciled = reconciled + step_size * direction
        residual = residual - step_size * image
        norm_next = squares(residual)
        direction = residual + norm_next / norm_now * direction
        norm_now = norm_next
    return (reconciled, residual)


def solution(mesh):
    in_specs = (
        P(("store", "sku"), None, None),
        P(("store", "sku"), None, None),
        P(("store", "sku"), None, None),
        P(("store", "sku"), None, None),
        P(None, None, ("store", "sku")),
        P(None, None, ("store", "sku")),
        P(),
        P(),
    )
    out_specs = (P(("store", "sku"), None, None), P(("store", "sku"), None, None))
    return jax.shard_map(
        on_device, mesh=mesh, in_specs=in_specs, out_specs=out_specs, check_vma=False
    )
```

profile of v0, /device:TPU:1, one launch (start us, length us, event | category | flops | bytes accessed | tf_op | source)
XLA Modules:
  0.0 1191.2 jit_solution(167319318847375889)
XLA Ops:
  0.6 15.4 %copy.158 = f32[1,13,16384]{1,0,2:T(1,128)} copy(f32[1,13,16384]{2,0,1:T(1,128)} %param.24) | data formatting | bytes 1703936 | tf_op args[0]
  16.6 74.5 %reduce.2 = f32[16384,13]{1,0:T(8,128)} reduce(f32[16384,1,13]{2,1,0:T(1,128)} %bitcast.248, f32[]{:T(128)} %broadcast.52), dimensions={1}, to_apply=%bitcast.187.reduce_sub_computation | reduce | bytes 1703940
  112.5 22.1 %while.116 = (s32[]{:T(128)}, f32[13,1024]{1,0:T(8,128)S(1)}, f32[13,16384]{1,0:T(8,128)S(1)}, s32[16384]{0:T(1024)S(1)}, s32[]{:T(128)}, /*index=5*/s32[]{:T(128)}, s32[]{:T(128)}, s32[]{:T(128)}) while((s32[]{:T(128)}, f32[13,1024]{1,0:T(8,128)S(1)}, f32[13,16384]{1,0:T(8,128)S(1)}, s32[16384]{0:T(1024)S(1)}, s32[]{:T(128)}, ...), condition=%wide.region_1.0_spmd.clone, body=%wide.region_0.0_spmd.clone.sunk | while | flops 329279488 | bytes 274581 | solution.py:32
  152.0 15.1 %copy.159 = f32[1,13,16384]{2,0,1:T(1,128)S(1)} copy(f32[1,13,16384]{1,0,2:T(1,128)} %bitcast.249) | data formatting | bytes 1703936 | tf_op jit(solution)/shard_map/all_to_all | solution.py:57
  180.4 21.7 %while.112 = (s32[]{:T(128)}, f32[13,16384]{1,0:T(8,128)S(1)}, s32[16384]{0:T(1024)S(1)}, f32[13,1024]{1,0:T(8,128)S(1)}, s32[]{:T(128)}, /*index=5*/s32[]{:T(128)}, s32[]{:T(128)}, s32[]{:T(128)}) while((s32[]{:T(128)}, f32[13,16384]{1,0:T(8,128)S(1)}, s32[16384]{0:T(1024)S(1)}, f32[13,1024]{1,0:T(8,128)S(1)}, s32[]{:T(128)}, ...), condition=%wide.region_3.0_spmd.clone, body=%wide.region_2.0_spmd.clone.sunk | while | flops 329252864 | bytes 221323 | solution.py:52
  216.2 74.5 %reduce.4 = f32[16384,13]{1,0:T(8,128)} reduce(f32[16384,1,13]{2,1,0:T(1,128)} %bitcast.245, f32[]{:T(128)} %broadcast.52), dimensions={1}, to_apply=%bitcast.189.reduce_sub_computation | reduce | bytes 1703940
  309.7 22.1 %while.117 = (s32[]{:T(128)}, f32[13,1024]{1,0:T(8,128)S(1)}, f32[13,16384]{1,0:T(8,128)S(1)}, s32[16384]{0:T(1024)S(1)}, s32[]{:T(128)}, /*index=5*/s32[]{:T(128)}, s32[]{:T(128)}, s32[]{:T(128)}) while((s32[]{:T(128)}, f32[13,1024]{1,0:T(8,128)S(1)}, f32[13,16384]{1,0:T(8,128)S(1)}, s32[16384]{0:T(1024)S(1)}, s32[]{:T(128)}, ...), condition=%wide.region_7.0_spmd.clone, body=%wide.region_6.0_spmd.clone.sunk | while | flops 329279488 | bytes 274581 | solution.py:32
  377.9 21.7 %while.113 = (s32[]{:T(128)}, f32[13,16384]{1,0:T(8,128)S(1)}, s32[16384]{0:T(1024)S(1)}, f32[13,1024]{1,0:T(8,128)S(1)}, s32[]{:T(128)}, /*index=5*/s32[]{:T(128)}, s32[]{:T(128)}, s32[]{:T(128)}) while((s32[]{:T(128)}, f32[13,16384]{1,0:T(8,128)S(1)}, s32[16384]{0:T(1024)S(1)}, f32[13,1024]{1,0:T(8,128)S(1)}, s32[]{:T(128)}, ...), condition=%wide.region_9.0_spmd.clone, body=%wide.region_8.0_spmd.clone.sunk | while | flops 329252864 | bytes 221323 | solution.py:52
  404.7 67.3 %all-reduce = (f32[]{:T(128)}, f32[]{:T(128)}) all-reduce(f32[]{:T(128)} %get-tuple-element.960, f32[]{:T(128)} %multiply_reduce_fusion.4), channel_id=1, replica_groups=mesh['store'=8,'sku'=16] {'store','sku'}, use_global_device_ids=true, to_apply=%region_5.0 | all-reduce | flops 2 | bytes 16 | tf_op jit(solution)/shard_map/psum | solution.py:65
  476.8 62.9 %psum.44 = f32[]{:T(128)} all-reduce(f32[]{:T(128)} %get-tuple-element.958), channel_id=1, replica_groups=mesh['store'=8,'sku'=16] {'store','sku'}, use_global_device_ids=true, to_apply=%region_13.0 | all-reduce | flops 1 | bytes 8 | tf_op jit(solution)/shard_map/psum | solution.py:65
  554.5 74.6 %reduce.6 = f32[16384,13]{1,0:T(8,128)} reduce(f32[16384,1,13]{2,1,0:T(1,128)} %bitcast.246, f32[]{:T(128)} %broadcast.52), dimensions={1}, to_apply=%bitcast.191.reduce_sub_computation | reduce | bytes 1703940
  644.6 22.1 %while.118 = (s32[]{:T(128)}, f32[13,1024]{1,0:T(8,128)S(1)}, f32[13,16384]{1,0:T(8,128)S(1)}, s32[16384]{0:T(1024)S(1)}, s32[]{:T(128)}, /*index=5*/s32[]{:T(128)}, s32[]{:T(128)}, s32[]{:T(128)}) while((s32[]{:T(128)}, f32[13,1024]{1,0:T(8,128)S(1)}, f32[13,16384]{1,0:T(8,128)S(1)}, s32[16384]{0:T(1024)S(1)}, s32[]{:T(128)}, ...), condition=%wide.region_15.0_spmd.clone, body=%wide.region_14.0_spmd.clone.sunk | while | flops 329279488 | bytes 274581 | solution.py:32
  671.6 15.5 %reshape.143 = f32[16384,1,13]{2,1,0:T(1,128)} reshape(f32[128,1664]{1,0:T(8,128)} %reduce.7) | data formatting | bytes 1703936
  687.1 16.3 %copy.178 = f32[1,13,16384]{2,0,1:T(1,128)} copy(f32[1,13,16384]{1,0,2:T(1,128)} %bitcast.251) | data formatting | bytes 1703936 | tf_op jit(solution)/shard_map/all_to_all | solution.py:57
  721.2 26.8 %while.114 = (s32[]{:T(128)}, f32[13,16384]{1,0:T(8,128)}, s32[16384]{0:T(1024)S(1)}, f32[13,1024]{1,0:T(8,128)S(1)}, s32[]{:T(128)}, /*index=5*/s32[]{:T(128)}, s32[]{:T(128)}, s32[]{:T(128)}) while((s32[]{:T(128)}, f32[13,16384]{1,0:T(8,128)}, s32[16384]{0:T(1024)S(1)}, f32[13,1024]{1,0:T(8,128)S(1)}, s32[]{:T(128)}, ...), condition=%wide.region_17.0_spmd.clone, body=%wide.region_16.0_spmd.clone.sunk | while | flops 329252864 | bytes 209035 | solution.py:52
  753.6 67.2 %psum.45 = f32[]{:T(128)} all-reduce(f32[]{:T(128)} %multiply_reduce_fusion.2), channel_id=1, replica_groups=mesh['store'=8,'sku'=16] {'store','sku'}, use_global_device_ids=true, to_apply=%region_19.0 | all-reduce | flops 1 | bytes 8 | tf_op jit(solution)/shard_map/psum | solution.py:107
  826.2 62.9 %psum.46 = f32[]{:T(128)} all-reduce(f32[]{:T(128)} %get-tuple-element.956), channel_id=1, replica_groups=mesh['store'=8,'sku'=16] {'store','sku'}, use_global_device_ids=true, to_apply=%region_21.0 | all-reduce | flops 1 | bytes 8 | tf_op jit(solution)/shard_map/psum | solution.py:65
  892.8 15.6 %copy.186 = f32[1,13,16384]{1,0,2:T(1,128)} copy(f32[1,13,16384]{2,1,0:T(8,128)} %multiply_add_fusion) | data formatting | bytes 1703936 | tf_op jit(solution)/shard_map/add | solution.py:111
  908.4 74.6 %reduce.8 = f32[16384,13]{1,0:T(8,128)} reduce(f32[16384,1,13]{2,1,0:T(1,128)} %bitcast.247, f32[]{:T(128)} %broadcast.52), dimensions={1}, to_apply=%bitcast.193.reduce_sub_computation | reduce | bytes 1703940
  998.2 29.3 %while.119 = (s32[]{:T(128)}, f32[13,1024]{1,0:T(8,128)S(1)}, f32[13,16384]{1,0:T(8,128)}, s32[16384]{0:T(1024)S(1)}, s32[]{:T(128)}, /*index=5*/s32[]{:T(128)}, s32[]{:T(128)}, s32[]{:T(128)}) while((s32[]{:T(128)}, f32[13,1024]{1,0:T(8,128)S(1)}, f32[13,16384]{1,0:T(8,128)}, s32[16384]{0:T(1024)S(1)}, s32[]{:T(128)}, ...), condition=%wide.region_23.0_spmd.clone, body=%wide.region_22.0_spmd.clone.sunk | while | flops 329279488 | bytes 262293 | solution.py:32
  1032.4 15.5 %reshape.145 = f32[16384,1,13]{2,1,0:T(1,128)} reshape(f32[128,1664]{1,0:T(8,128)} %reduce.9) | data formatting | bytes 1703936
  1047.9 16.3 %copy.187 = f32[1,13,16384]{2,0,1:T(1,128)} copy(f32[1,13,16384]{1,0,2:T(1,128)} %bitcast.252) | data formatting | bytes 1703936 | tf_op jit(solution)/shard_map/all_to_all | solution.py:57
  1082.1 26.8 %while.115 = (s32[]{:T(128)}, f32[13,16384]{1,0:T(8,128)}, s32[16384]{0:T(1024)S(1)}, f32[13,1024]{1,0:T(8,128)S(1)}, s32[]{:T(128)}, /*index=5*/s32[]{:T(128)}, s32[]{:T(128)}, s32[]{:T(128)}) while((s32[]{:T(128)}, f32[13,16384]{1,0:T(8,128)}, s32[16384]{0:T(1024)S(1)}, f32[13,1024]{1,0:T(8,128)S(1)}, s32[]{:T(128)}, ...), condition=%wide.region_25.0_spmd.clone, body=%wide.region_24.0_spmd.clone.sunk | while | flops 329252864 | bytes 209035 | solution.py:52
  1114.9 67.2 %psum.47 = f32[]{:T(128)} all-reduce(f32[]{:T(128)} %multiply_reduce_fusion), channel_id=1, replica_groups=mesh['store'=8,'sku'=16] {'store','sku'}, use_global_device_ids=true, to_apply=%region_27.0 | all-reduce | flops 1 | bytes 8 | tf_op jit(solution)/shard_map/psum | solution.py:107
  (232 shorter events, 447.2 us)
Async XLA Ops:
  91.1 20.8 %copy-start.4 = (f32[1,13,16384]{2,0,1:T(1,128)S(1)}, f32[1,13,16384]{2,0,1:T(1,128)}, u32[]{:S(2)}) copy-start(f32[1,13,16384]{2,0,1:T(1,128)} %param.24) | copy-start | bytes 2555908
  91.1 21.3 %copy-start.6 = (s32[16384]{0:T(1024)S(1)}, s32[16384]{0:T(1024)}, u32[]{:S(2)}) copy-start(s32[16384]{0:T(1024)} %param.30) | copy-start | bytes 196612
  100.1 34.5 %copy-start.7 = (f32[1,13,1024]{2,0,1:T(1,128)S(1)}, f32[1,13,1024]{2,0,1:T(1,128)}, u32[]{:S(2)}) copy-start(f32[1,13,1024]{2,0,1:T(1,128)} %param.27) | copy-start | bytes 159748
  100.1 34.5 %copy-start.9 = (f32[1,13,1024]{2,0,1:T(1,128)S(1)}, f32[1,13,1024]{2,0,1:T(1,128)}, u32[]{:S(2)}) copy-start(f32[1,13,1024]{2,0,1:T(1,128)} %param.26) | copy-start | bytes 159748
  100.1 34.5 %all-to-all-start = ((f32[128,1,1664]{2,1,0:T(1,128)}), f32[128,1,1664]{2,1,0:T(1,128)S(1)}, u32[]{:S(2)}, u32[]{:S(2)}) async-start(f32[128,1,1664]{2,1,0:T(1,128)} %reshape.138), calls=%async_computation | async-start | bytes 1703936 | tf_op jit(solution)/shard_map/all_to_all | solution.py:57
  137.4 30.0 %copy-start.5 = (f32[32,13,128]{2,0,1:T(8,128)S(1)}, f32[32,13,128]{2,0,1:T(8,128)}, u32[]{:S(2)}) copy-start(f32[32,13,128]{2,0,1:T(8,128)} %param.29) | copy-start | bytes 638980
  137.4 30.0 %copy-start.8 = (f32[32,13,128]{2,0,1:T(8,128)S(1)}, f32[32,13,128]{2,0,1:T(8,128)}, u32[]{:S(2)}) copy-start(f32[32,13,128]{2,0,1:T(8,128)} %param.28) | copy-start | bytes 638980
  137.4 30.0 %copy-start.10 = (s32[128]{0:T(128)S(1)}, s32[128]{0:T(128)}, u32[]{:S(2)}) copy-start(s32[128]{0:T(128)} %param.31) | copy-start | bytes 1540
  170.1 32.1 %all-to-all-start.1 = ((f32[128,13,128]{2,1,0:T(8,128)}), f32[128,13,128]{2,1,0:T(8,128)S(1)}, u32[]{:S(2)}, u32[]{:S(2)}) async-start(f32[128,13,128]{2,1,0:T(8,128)} %copy.163), calls=%async_computation.1 | async-start | bytes 2097152 | tf_op jit(solution)/shard_map/all_to_all | solution.py:61
  299.7 32.2 %all-to-all-start.2 = ((f32[128,1,1664]{2,1,0:T(1,128)}), f32[128,1,1664]{2,1,0:T(1,128)S(1)}, u32[]{:S(2)}, u32[]{:S(2)}) async-start(f32[128,1,1664]{2,1,0:T(1,128)} %reshape.140), calls=%async_computation.2 | async-start | bytes 1703936 | tf_op jit(solution)/shard_map/all_to_all | solution.py:57
  367.2 32.5 %all-to-all-start.3 = ((f32[128,13,128]{2,1,0:T(8,128)}), f32[128,13,128]{2,1,0:T(8,128)}, u32[]{:S(2)}, u32[]{:S(2)}) async-start(f32[128,13,128]{2,1,0:T(8,128)} %copy.172), calls=%async_computation.3 | async-start | bytes 2097152 | tf_op jit(solution)/shard_map/all_to_all | solution.py:61
  377.9 24.4 %copy-start = (f32[1,13,16384]{2,0,1:T(1,128)S(1)}, f32[1,13,16384]{2,0,1:T(1,128)}, u32[]{:S(2)}) copy-start(f32[1,13,16384]{2,0,1:T(1,128)} %param.25) | copy-start | bytes 2555908
  399.7 2.0 copy-start.2
  638.1 28.7 %all-to-all-start.4 = ((f32[128,1,1664]{2,1,0:T(1,128)}), f32[128,1,1664]{2,1,0:T(1,128)}, u32[]{:S(2)}, u32[]{:S(2)}) async-start(f32[128,1,1664]{2,1,0:T(1,128)} %reshape.142), calls=%async_computation.4 | async-start | bytes 1703936 | tf_op jit(solution)/shard_map/all_to_all | solution.py:57
  709.5 38.4 %all-to-all-start.5 = ((f32[128,13,128]{2,1,0:T(8,128)}), f32[128,13,128]{2,1,0:T(8,128)}, u32[]{:S(2)}, u32[]{:S(2)}) async-start(f32[128,13,128]{2,1,0:T(8,128)} %copy.182), calls=%async_computation.5 | async-start | bytes 2097152 | tf_op jit(solution)/shard_map/all_to_all | solution.py:61
  750.2 1.0 copy-start.1
  991.9 35.7 %all-to-all-start.6 = ((f32[128,1,1664]{2,1,0:T(1,128)}), f32[128,1,1664]{2,1,0:T(1,128)}, u32[]{:S(2)}, u32[]{:S(2)}) async-start(f32[128,1,1664]{2,1,0:T(1,128)} %reshape.144), calls=%async_computation.6 | async-start | bytes 1703936 | tf_op jit(solution)/shard_map/all_to_all | solution.py:57
  1070.3 38.6 %all-to-all-start.7 = ((f32[128,13,128]{2,1,0:T(8,128)}), f32[128,13,128]{2,1,0:T(8,128)}, u32[]{:S(2)}, u32[]{:S(2)}) async-start(f32[128,13,128]{2,1,0:T(8,128)} %copy.191), calls=%async_computation.7 | async-start | bytes 2097152 | tf_op jit(solution)/shard_map/all_to_all | solution.py:61
  1111.1 1.0 copy-start.3
where the time goes:
time: 1200 us; the launch traced here: 1190 us
  other arithmetic  337 us (28%)
  blocking collectives  327 us (27%)
  local copies, waits for them, and re-layouts  242 us (20%)
  matrix products  199 us (17%)
  starting transfers between devices  77 us (6%)
    unnamed x8, other arithmetic  298 us
    psum x3, blocking collectives, squares(): return lax.psum(jnp.sum(residual * residual), ('store', 'sku'))  193 us
    psum x2, blocking collectives, on_device(): lax.psum(jnp.sum(direction * image), ('store', 'sku'))  134 us
    unnamed x43, local copies, waits for them, and re-layouts  121 us
    dot_general x32, matrix products, place(): jnp.dot(flat, onehot, precision=lax.Precision.HIGHEST, preferred_element_...  96.7 us
    dot_general x32, matrix products, accumulate(): jnp.dot(columns, onehot, precision=lax.Precision.HIGHEST, preferred_eleme...  95.5 us
    all_to_all x8, local copies, waits for them, and re-layouts, to_region(): lax.all_to_all(field, ('store', 'sku'), split_axis=2, concat_axis=0, tile...  68.1 us
    all_to_all x4, starting transfers between devices, from_region(): lax.all_to_all(field, ('store', 'sku'), split_axis=0, concat_axis=2, tile...  42.2 us
  transfers between devices with their start and end apart: 8, of which 0 were waited for; matrix products, arithmetic and copies ran while one was open for 16% of the time, Pallas kernels for 0%

commit v1 on v0

--- a/solution.py
+++ b/solution.py
@@ -58,7 +58,15 @@
 
 
 def from_region(field):
-    return lax.all_to_all(field, ("store", "sku"), split_axis=0, concat_axis=2, tiled=True)
+    return jnp.concatenate(
+        lax.all_to_all(
+            jnp.stack(jnp.split(field, lax.axis_size(("store", "sku")), axis=0)),
+            ("store", "sku"),
+            0,
+            0,
+        ),
+        axis=2,
+    )
 
 
 def squares(residual):

time: 1200 us -> 1220 us (1.017)
  local copies, waits for them, and re-layouts: 242 us -> 255 us
    unnamed x43 -> x551, local copies, waits for them, and re-layouts: 121 us -> 122 us
where the time goes in v1:
time: 1220 us; the launch traced here: 1200 us
  other arithmetic  336 us (28%)
  blocking collectives  328 us (27%)
  local copies, waits for them, and re-layouts  255 us (21%)
  matrix products  199 us (16%)
  starting transfers between devices  75.2 us (6%)
    unnamed x8, other arithmetic  298 us
    psum x3, blocking collectives, squares(): return lax.psum(jnp.sum(residual * residual), ('store', 'sku'))  193 us
    psum x2, blocking collectives, on_device(): lax.psum(jnp.sum(direction * image), ('store', 'sku'))  135 us
    unnamed x551, local copies, waits for them, and re-layouts  122 us
    dot_general x32, matrix products, place(): jnp.dot(flat, onehot, precision=lax.Precision.HIGHEST, preferred_element_...  96.8 us
    dot_general x32, matrix products, accumulate(): jnp.dot(columns, onehot, precision=lax.Precision.HIGHEST, preferred_eleme...  95.5 us
    all_to_all x8, local copies, waits for them, and re-layouts, to_region(): lax.all_to_all(field, ('store', 'sku'), split_axis=2, concat_axis=0, tile...  69.7 us
    all_to_all x4, starting transfers between devices, from_region(): lax.all_to_all(jnp.stack(jnp.split(field, lax.axis_size(('store', 'sku'))...  40.5 us
  transfers between devices with their start and end apart: 8, of which 0 were waited for; matrix products, arithmetic and copies ran while one was open for 16% of the time, Pallas kernels for 0%

profile of v1, /device:TPU:1, one launch (start us, length us, event | category | flops | bytes accessed | tf_op | source)
XLA Modules:
  0.0 1204.9 jit_solution(11165120549861597428)
XLA Ops:
  16.5 74.4 %reduce.1026 = f32[16384,13]{1,0:T(8,128)} reduce(f32[16384,1,13]{2,1,0:T(1,128)} %bitcast.1222, f32[]{:T(128)} %broadcast.564), dimensions={1}, to_apply=%bitcast.1177.reduce_sub_computation | reduce | bytes 1703940
  112.4 22.1 %while.116 = (s32[]{:T(128)}, f32[13,1024]{1,0:T(8,128)S(1)}, f32[13,16384]{1,0:T(8,128)S(1)}, s32[16384]{0:T(1024)S(1)}, s32[]{:T(128)}, /*index=5*/s32[]{:T(128)}, s32[]{:T(128)}, s32[]{:T(128)}) while((s32[]{:T(128)}, f32[13,1024]{1,0:T(8,128)S(1)}, f32[13,16384]{1,0:T(8,128)S(1)}, s32[16384]{0:T(1024)S(1)}, s32[]{:T(128)}, ...), condition=%wide.region_1.0_spmd.clone, body=%wide.region_0.0_spmd.clone.sunk | while | flops 329279488 | bytes 274581 | solution.py:32
  151.9 15.7 %copy.214 = f32[1,13,16384]{2,0,1:T(1,128)S(1)} copy(f32[1,13,16384]{1,0,2:T(1,128)} %bitcast.1223) | data formatting | bytes 1703936 | tf_op jit(solution)/shard_map/all_to_all | solution.py:57
  184.7 21.7 %while.112 = (s32[]{:T(128)}, f32[13,16384]{1,0:T(8,128)S(1)}, s32[16384]{0:T(1024)S(1)}, f32[13,1024]{1,0:T(8,128)S(1)}, s32[]{:T(128)}, /*index=5*/s32[]{:T(128)}, s32[]{:T(128)}, s32[]{:T(128)}) while((s32[]{:T(128)}, f32[13,16384]{1,0:T(8,128)S(1)}, s32[16384]{0:T(1024)S(1)}, f32[13,1024]{1,0:T(8,128)S(1)}, s32[]{:T(128)}, ...), condition=%wide.region_3.0_spmd.clone, body=%wide.region_2.0_spmd.clone.sunk | while | flops 329252864 | bytes 221323 | solution.py:52
  220.2 74.4 %reduce.1028 = f32[16384,13]{1,0:T(8,128)} reduce(f32[16384,1,13]{2,1,0:T(1,128)} %bitcast.1219, f32[]{:T(128)} %broadcast.564), dimensions={1}, to_apply=%bitcast.1179.reduce_sub_computation | reduce | bytes 1703940
  313.7 22.1 %while.117 = (s32[]{:T(128)}, f32[13,1024]{1,0:T(8,128)S(1)}, f32[13,16384]{1,0:T(8,128)S(1)}, s32[16384]{0:T(1024)S(1)}, s32[]{:T(128)}, /*index=5*/s32[]{:T(128)}, s32[]{:T(128)}, s32[]{:T(128)}) while((s32[]{:T(128)}, f32[13,1024]{1,0:T(8,128)S(1)}, f32[13,16384]{1,0:T(8,128)S(1)}, s32[16384]{0:T(1024)S(1)}, s32[]{:T(128)}, ...), condition=%wide.region_7.0_spmd.clone, body=%wide.region_6.0_spmd.clone.sunk | while | flops 329279488 | bytes 274581 | solution.py:32
  353.0 15.5 %copy.222 = f32[1,13,16384]{2,0,1:T(1,128)S(1)} copy(f32[1,13,16384]{1,0,2:T(1,128)} %bitcast.1224) | data formatting | bytes 1703936 | tf_op jit(solution)/shard_map/all_to_all | solution.py:57
  385.7 21.7 %while.113 = (s32[]{:T(128)}, f32[13,16384]{1,0:T(8,128)S(1)}, s32[16384]{0:T(1024)S(1)}, f32[13,1024]{1,0:T(8,128)S(1)}, s32[]{:T(128)}, /*index=5*/s32[]{:T(128)}, s32[]{:T(128)}, s32[]{:T(128)}) while((s32[]{:T(128)}, f32[13,16384]{1,0:T(8,128)S(1)}, s32[16384]{0:T(1024)S(1)}, f32[13,1024]{1,0:T(8,128)S(1)}, s32[]{:T(128)}, ...), condition=%wide.region_9.0_spmd.clone, body=%wide.region_8.0_spmd.clone.sunk | while | flops 329252864 | bytes 221323 | solution.py:52
  412.2 67.4 %all-reduce = (f32[]{:T(128)}, f32[]{:T(128)}) all-reduce(f32[]{:T(128)} %get-tuple-element.1466, f32[]{:T(128)} %multiply_reduce_fusion.4), channel_id=1, replica_groups=mesh['store'=8,'sku'=16] {'store','sku'}, use_global_device_ids=true, to_apply=%region_5.0 | all-reduce | flops 2 | bytes 16 | tf_op jit(solution)/shard_map/psum | solution.py:73
  484.5 62.6 %psum.44 = f32[]{:T(128)} all-reduce(f32[]{:T(128)} %get-tuple-element.1464), channel_id=1, replica_groups=mesh['store'=8,'sku'=16] {'store','sku'}, use_global_device_ids=true, to_apply=%region_13.0 | all-reduce | flops 1 | bytes 8 | tf_op jit(solution)/shard_map/psum | solution.py:73
  561.8 74.4 %reduce.1030 = f32[16384,13]{1,0:T(8,128)} reduce(f32[16384,1,13]{2,1,0:T(1,128)} %bitcast.1220, f32[]{:T(128)} %broadcast.564), dimensions={1}, to_apply=%bitcast.1181.reduce_sub_computation | reduce | bytes 1703940
  651.5 22.1 %while.118 = (s32[]{:T(128)}, f32[13,1024]{1,0:T(8,128)S(1)}, f32[13,16384]{1,0:T(8,128)S(1)}, s32[16384]{0:T(1024)S(1)}, s32[]{:T(128)}, /*index=5*/s32[]{:T(128)}, s32[]{:T(128)}, s32[]{:T(128)}) while((s32[]{:T(128)}, f32[13,1024]{1,0:T(8,128)S(1)}, f32[13,16384]{1,0:T(8,128)S(1)}, s32[16384]{0:T(1024)S(1)}, s32[]{:T(128)}, ...), condition=%wide.region_15.0_spmd.clone, body=%wide.region_14.0_spmd.clone.sunk | while | flops 329279488 | bytes 274581 | solution.py:32
  678.3 15.5 %reshape.1706 = f32[16384,1,13]{2,1,0:T(1,128)} reshape(f32[128,1664]{1,0:T(8,128)} %reduce.1031) | data formatting | bytes 1703936
  693.8 16.7 %copy.231 = f32[1,13,16384]{2,0,1:T(1,128)} copy(f32[1,13,16384]{1,0,2:T(1,128)} %bitcast.1225) | data formatting | bytes 1703936 | tf_op jit(solution)/shard_map/all_to_all | solution.py:57
  731.9 26.8 %while.114 = (s32[]{:T(128)}, f32[13,16384]{1,0:T(8,128)}, s32[16384]{0:T(1024)S(1)}, f32[13,1024]{1,0:T(8,128)S(1)}, s32[]{:T(128)}, /*index=5*/s32[]{:T(128)}, s32[]{:T(128)}, s32[]{:T(128)}) while((s32[]{:T(128)}, f32[13,16384]{1,0:T(8,128)}, s32[16384]{0:T(1024)S(1)}, f32[13,1024]{1,0:T(8,128)S(1)}, s32[]{:T(128)}, ...), condition=%wide.region_17.0_spmd.clone, body=%wide.region_16.0_spmd.clone.sunk | while | flops 329252864 | bytes 209035 | solution.py:52
  764.1 67.3 %psum.45 = f32[]{:T(128)} all-reduce(f32[]{:T(128)} %multiply_reduce_fusion.2), channel_id=1, replica_groups=mesh['store'=8,'sku'=16] {'store','sku'}, use_global_device_ids=true, to_apply=%region_19.0 | all-reduce | flops 1 | bytes 8 | tf_op jit(solution)/shard_map/psum | solution.py:115
  836.8 62.7 %psum.46 = f32[]{:T(128)} all-reduce(f32[]{:T(128)} %get-tuple-element.1462), channel_id=1, replica_groups=mesh['store'=8,'sku'=16] {'store','sku'}, use_global_device_ids=true, to_apply=%region_21.0 | all-reduce | flops 1 | bytes 8 | tf_op jit(solution)/shard_map/psum | solution.py:73
  903.0 15.6 %copy.238 = f32[1,13,16384]{1,0,2:T(1,128)} copy(f32[1,13,16384]{2,1,0:T(8,128)} %multiply_add_fusion) | data formatting | bytes 1703936 | tf_op jit(solution)/shard_map/add | solution.py:119
  918.6 74.4 %reduce.1032 = f32[16384,13]{1,0:T(8,128)} reduce(f32[16384,1,13]{2,1,0:T(1,128)} %bitcast.1221, f32[]{:T(128)} %broadcast.564), dimensions={1}, to_apply=%bitcast.1183.reduce_sub_computation | reduce | bytes 1703940
  1008.3 29.3 %while.119 = (s32[]{:T(128)}, f32[13,1024]{1,0:T(8,128)S(1)}, f32[13,16384]{1,0:T(8,128)}, s32[16384]{0:T(1024)S(1)}, s32[]{:T(128)}, /*index=5*/s32[]{:T(128)}, s32[]{:T(128)}, s32[]{:T(128)}) while((s32[]{:T(128)}, f32[13,1024]{1,0:T(8,128)S(1)}, f32[13,16384]{1,0:T(8,128)}, s32[16384]{0:T(1024)S(1)}, s32[]{:T(128)}, ...), condition=%wide.region_23.0_spmd.clone, body=%wide.region_22.0_spmd.clone.sunk | while | flops 329279488 | bytes 262293 | solution.py:32
  1042.3 15.5 %reshape.1708 = f32[16384,1,13]{2,1,0:T(1,128)} reshape(f32[128,1664]{1,0:T(8,128)} %reduce.1033) | data formatting | bytes 1703936
  1057.8 16.5 %copy.239 = f32[1,13,16384]{2,0,1:T(1,128)} copy(f32[1,13,16384]{1,0,2:T(1,128)} %bitcast.1226) | data formatting | bytes 1703936 | tf_op jit(solution)/shard_map/all_to_all | solution.py:57
  1095.8 26.8 %while.115 = (s32[]{:T(128)}, f32[13,16384]{1,0:T(8,128)}, s32[16384]{0:T(1024)S(1)}, f32[13,1024]{1,0:T(8,128)S(1)}, s32[]{:T(128)}, /*index=5*/s32[]{:T(128)}, s32[]{:T(128)}, s32[]{:T(128)}) while((s32[]{:T(128)}, f32[13,16384]{1,0:T(8,128)}, s32[16384]{0:T(1024)S(1)}, f32[13,1024]{1,0:T(8,128)S(1)}, s32[]{:T(128)}, ...), condition=%wide.region_25.0_spmd.clone, body=%wide.region_24.0_spmd.clone.sunk | while | flops 329252864 | bytes 209035 | solution.py:52
  1128.3 67.5 %psum.47 = f32[]{:T(128)} all-reduce(f32[]{:T(128)} %multiply_reduce_fusion), channel_id=1, replica_groups=mesh['store'=8,'sku'=16] {'store','sku'}, use_global_device_ids=true, to_apply=%region_27.0 | all-reduce | flops 1 | bytes 8 | tf_op jit(solution)/shard_map/psum | solution.py:115
  (772 shorter events, 456.2 us)
Async XLA Ops:
  91.0 21.0 %copy-start.4 = (f32[1,13,16384]{2,0,1:T(1,128)S(1)}, f32[1,13,16384]{2,0,1:T(1,128)}, u32[]{:S(2)}) copy-start(f32[1,13,16384]{2,0,1:T(1,128)} %param.24) | copy-start | bytes 2555908
  91.0 21.5 %copy-start.6 = (s32[16384]{0:T(1024)S(1)}, s32[16384]{0:T(1024)}, u32[]{:S(2)}) copy-start(s32[16384]{0:T(1024)} %param.30) | copy-start | bytes 196612
  100.0 34.6 %copy-start.7 = (f32[1,13,1024]{2,0,1:T(1,128)S(1)}, f32[1,13,1024]{2,0,1:T(1,128)}, u32[]{:S(2)}) copy-start(f32[1,13,1024]{2,0,1:T(1,128)} %param.27) | copy-start | bytes 159748
  100.0 34.6 %copy-start.9 = (f32[1,13,1024]{2,0,1:T(1,128)S(1)}, f32[1,13,1024]{2,0,1:T(1,128)}, u32[]{:S(2)}) copy-start(f32[1,13,1024]{2,0,1:T(1,128)} %param.26) | copy-start | bytes 159748
  100.0 34.6 %all-to-all-start = ((f32[128,1,1664]{2,1,0:T(1,128)}), f32[128,1,1664]{2,1,0:T(1,128)S(1)}, u32[]{:S(2)}, u32[]{:S(2)}) async-start(f32[128,1,1664]{2,1,0:T(1,128)} %reshape.1701), calls=%async_computation | async-start | bytes 1703936 | tf_op jit(solution)/shard_map/all_to_all | solution.py:57
  137.3 30.6 %copy-start.5 = (f32[32,13,128]{2,0,1:T(8,128)S(1)}, f32[32,13,128]{2,0,1:T(8,128)}, u32[]{:S(2)}) copy-start(f32[32,13,128]{2,0,1:T(8,128)} %param.29) | copy-start | bytes 638980
  137.3 30.6 %copy-start.8 = (f32[32,13,128]{2,0,1:T(8,128)S(1)}, f32[32,13,128]{2,0,1:T(8,128)}, u32[]{:S(2)}) copy-start(f32[32,13,128]{2,0,1:T(8,128)} %param.28) | copy-start | bytes 638980
  137.3 30.6 %copy-start.10 = (s32[128]{0:T(128)S(1)}, s32[128]{0:T(128)}, u32[]{:S(2)}) copy-start(s32[128]{0:T(128)} %param.31) | copy-start | bytes 1540
  174.5 31.9 %all-to-all-start.1 = ((f32[128,1,13,128]{3,1,2,0:T(1,128)}), f32[128,1,13,128]{3,1,2,0:T(1,128)S(1)}, u32[]{:S(2)}, u32[]{:S(2)}) async-start(f32[128,1,13,128]{3,1,2,0:T(1,128)} %copy.217), calls=%async_computation.1 | async-start | bytes 1703936 | tf_op jit(solution)/shard_map/all_to_all | solution.py:62
  303.6 32.2 %all-to-all-start.2 = ((f32[128,1,1664]{2,1,0:T(1,128)}), f32[128,1,1664]{2,1,0:T(1,128)S(1)}, u32[]{:S(2)}, u32[]{:S(2)}) async-start(f32[128,1,1664]{2,1,0:T(1,128)} %reshape.1703), calls=%async_computation.2 | async-start | bytes 1703936 | tf_op jit(solution)/shard_map/all_to_all | solution.py:57
  375.5 32.0 %all-to-all-start.3 = ((f32[128,1,13,128]{3,1,2,0:T(1,128)}), f32[128,1,13,128]{3,1,2,0:T(1,128)}, u32[]{:S(2)}, u32[]{:S(2)}) async-start(f32[128,1,13,128]{3,1,2,0:T(1,128)} %copy.225), calls=%async_computation.3 | async-start | bytes 1703936 | tf_op jit(solution)/shard_map/all_to_all | solution.py:62
  385.7 24.1 %copy-start = (f32[1,13,16384]{2,0,1:T(1,128)S(1)}, f32[1,13,16384]{2,0,1:T(1,128)}, u32[]{:S(2)}) copy-start(f32[1,13,16384]{2,0,1:T(1,128)} %param.25) | copy-start | bytes 2555908
  407.5 1.7 copy-start.2
  645.1 28.5 %all-to-all-start.4 = ((f32[128,1,1664]{2,1,0:T(1,128)}), f32[128,1,1664]{2,1,0:T(1,128)}, u32[]{:S(2)}, u32[]{:S(2)}) async-start(f32[128,1,1664]{2,1,0:T(1,128)} %reshape.1705), calls=%async_computation.4 | async-start | bytes 1703936 | tf_op jit(solution)/shard_map/all_to_all | solution.py:57
  720.6 38.1 %all-to-all-start.5 = ((f32[128,1,13,128]{3,1,2,0:T(1,128)}), f32[128,1,13,128]{3,1,2,0:T(1,128)}, u32[]{:S(2)}, u32[]{:S(2)}) async-start(f32[128,1,13,128]{3,1,2,0:T(1,128)} %copy.234), calls=%async_computation.5 | async-start | bytes 1703936 | tf_op jit(solution)/shard_map/all_to_all | solution.py:62
  760.7 1.0 copy-start.1
  1002.0 35.7 %all-to-all-start.6 = ((f32[128,1,1664]{2,1,0:T(1,128)}), f32[128,1,1664]{2,1,0:T(1,128)}, u32[]{:S(2)}, u32[]{:S(2)}) async-start(f32[128,1,1664]{2,1,0:T(1,128)} %reshape.1707), calls=%async_computation.6 | async-start | bytes 1703936 | tf_op jit(solution)/shard_map/all_to_all | solution.py:57
  1084.5 38.1 %all-to-all-start.7 = ((f32[128,1,13,128]{3,1,2,0:T(1,128)}), f32[128,1,13,128]{3,1,2,0:T(1,128)}, u32[]{:S(2)}, u32[]{:S(2)}) async-start(f32[128,1,13,128]{3,1,2,0:T(1,128)} %copy.242), calls=%async_computation.7 | async-start | bytes 1703936 | tf_op jit(solution)/shard_map/all_to_all | solution.py:62
  1124.6 1.0 copy-start.3
